TPU v7x, 512 devices: a whole 4x4x16 slice. The times are simulated.
512 devices in a mesh: band: 8 (over x, core), pw: 64 (over z, y).
Axes of the slice: x: 4, y: 4, z: 16, core: 2. Of those that a mesh axis runs over, the one named last changes fastest.
Arguments:
- orbital_coefficients: float32 [8, 2, 128, 128, 128], P('band', None, 'pw'), may hold values from -6 to 6
- sphere_halfwidth: int32 [128, 128], P('pw'), may hold values from -1 to 63, as said below
- occupation: float32 [8], P('band'), may hold values from 0.5 to 2
- local_potential: float32 [256, 256, 256], P(None, 'pw'), may hold values from -6 to 6
- stencil_corner: int32 [64, 64, 128], P('pw'), may hold values from 0 to 262143, as said below
- stencil_weight: float32 [8, 64, 64, 128], P(None, 'pw'), may hold values from -3 to 3
- point_count: int32 [64, 64], P('pw'), may hold values from 0 to 128, as said below
Outputs:
- local_action: float32 [8, 2, 128, 128, 128], P('band', None, 'pw')
- fit_potential: float32 [64, 64, 128], P('pw')
Inputs may be any that keep to these rules, and one draw needn't show every extreme that they name: `sphere_halfwidth`: in every draw the kept columns form one sphere centred at frequency zero that reaches the cube's faces; -1 marks an empty column. `stencil_corner`: each corner is x * 4 + y times 256 plus z, with x and z in 0 to 255 and y in 0 to 3. `point_count`: in every draw some tile has all 128 slots live from every source, and every source has some block with all 128 slots live.
All inputs are finite; a program needn't handle non-finite values.
Results may differ from a plain program's by a relative error of at most 0.0003.
Values sent between devices are 32-bit elements; how exact they have to be, the bound alone decides.
A program may use at most 64 MiB of HBM per device.

v0:
```python
import math
import jax
import jax.numpy as jnp
from jax import lax
from jax.sharding import PartitionSpec as P

hartree_scale = 200.0
exact_mode = lax.Precision.HIGHEST


def shifted(value, axis, steps):
    count = lax.axis_size(axis)
    pairs = [(source, (source + steps) % count) for source in range(count)]
    return lax.ppermute(value, axis, pairs)


def phases(frequency, grid_size):
    position = jnp.arange(grid_size, dtype=jnp.int32)
    product = jnp.remainder(frequency[:, None] * position[None, :], grid_size)
    angle = product.astype(jnp.float32) * (2.0 * math.pi / grid_size)
    return (jnp.cos(angle), jnp.sin(angle))


def inverse_table(frequency, grid_size):
    cosine, sine = phases(frequency, grid_size)
    from_real = jnp.stack([cosine, sine], axis=1)
    from_imag = jnp.stack([-sine, cosine], axis=1)
    return jnp.stack([from_real, from_imag], axis=0)


def forward_table(frequency, grid_size):
    cosine, sine = phases(frequency, grid_size)
    from_real = jnp.stack([cosine.T, -sine.T], axis=1)
    from_imag = jnp.stack([sine.T, cosine.T], axis=1)
    return jnp.stack([from_real, from_imag], axis=0)


def transform(operand, matrix, target_axis, component_axis):
    result = lax.dot_general(
        operand,
        matrix,
        (((component_axis, target_axis), (0, 1)), ((), ())),
        precision=exact_mode,
        preferred_element_type=jnp.float32,
    )
    dimensions = operand.ndim
    return jnp.moveaxis(result, (dimensions - 2, dimensions - 1), (component_axis, target_axis))


def kernel_values(start_x, count_x, start_y, count_y, grid_size):

    def signed(start, count):
        frequency = start + jnp.arange(count, dtype=jnp.int32)
        return jnp.where(frequency < grid_size // 2, frequency, frequency - grid_size)

    along_x = signed(start_x, count_x)
    along_y = signed(start_y, count_y)
    along_z = signed(0, grid_size)
    square = along_x[:, None, None] ** 2 + along_y[None, :, None] ** 2 + along_z[None, None, :] ** 2
    return jnp.where(square > 0, hartree_scale / jnp.maximum(square, 1).astype(jnp.float32), 0.0)


def body(
    orbital_coefficients,
    sphere_halfwidth,
    occupation,
    local_potential,
    stencil_corner,
    stencil_weight,
    point_count,
):
    cube_size = orbital_coefficients.shape[3]
    grid_size = local_potential.shape[0]
    slab_depth = local_potential.shape[1]
    slot_count = stencil_corner.shape[2]
    cube_freq = jnp.arange(cube_size, dtype=jnp.int32) - cube_size // 2
    sphere_mask = (jnp.abs(cube_freq)[None, None, :] <= sphere_halfwidth[:, :, None]).astype(
        jnp.float32
    )
    scale_in = float(cube_size) ** (-1.5)
    scale_out = float(cube_size) ** 1.5 / float(grid_size) ** 3
    inverse_cube = inverse_table(cube_freq, grid_size)
    forward_cube = forward_table(cube_freq, grid_size)
    coefficient = orbital_coefficients * (sphere_mask * scale_in)[None, None]
    partial_section = transform(coefficient, inverse_cube, 4, 1)
    partial_section = transform(partial_section, inverse_cube, 3, 1)
    orbital = transform(
        lax.all_to_all(partial_section, "pw", split_axis=3, concat_axis=2, tiled=True),
        inverse_cube,
        2,
        1,
    )
    partial_density = jnp.sum(
        occupation[:, None, None, None] * (orbital[:, 0] ** 2 + orbital[:, 1] ** 2), axis=0
    )
    product = orbital * local_potential[None, None]
    forward_section = transform(product, forward_cube, 2, 1)
    pencil = lax.all_to_all(forward_section, "pw", split_axis=2, concat_axis=3, tiled=True)
    pencil = transform(pencil, forward_cube, 3, 1)
    spectrum_cube = transform(pencil, forward_cube, 4, 1)
    local_action = spectrum_cube * (sphere_mask * scale_out)[None, None]
    grid_freq = jnp.arange(grid_size, dtype=jnp.int32)
    forward_grid = forward_table(grid_freq, grid_size)
    inverse_grid = inverse_table(grid_freq, grid_size)
    pw_count = lax.axis_size("pw")
    band_count = lax.axis_size("band")
    x_block = grid_size // pw_count
    x_start = lax.axis_index("pw") * x_block
    inverse_norm = 1.0 / float(grid_size) ** 3
    y_block = grid_size // band_count
    y_start = lax.axis_index("band") * y_block
    density_part = lax.psum_scatter(partial_density, "band", scatter_dimension=2, tiled=True)
    spectrum = transform(density_part[None], forward_grid[0:1], 1, 0)
    spectrum = lax.all_to_all(spectrum, "pw", split_axis=1, concat_axis=2, tiled=True)
    spectrum = transform(spectrum, forward_grid, 2, 0)
    spectrum = lax.all_to_all(spectrum, "band", split_axis=2, concat_axis=3, tiled=True)
    spectrum = transform(spectrum, forward_grid, 3, 0)
    spectrum = spectrum * kernel_values(x_start, x_block, y_start, y_block, grid_size)[None]
    spectrum = transform(spectrum, inverse_grid, 3, 0)
    spectrum = lax.all_to_all(spectrum, "band", split_axis=3, concat_axis=2, tiled=True)
    spectrum = transform(spectrum, inverse_grid, 2, 0)
    spectrum = lax.all_to_all(spectrum, "pw", split_axis=2, concat_axis=1, tiled=True)
    hartree_part = transform(spectrum, inverse_grid[:, :, 0:1], 1, 0)[0] * inverse_norm
    hartree = lax.all_gather(hartree_part, "band", axis=2, tiled=True)
    upper_plane = shifted(hartree[:, 0:1, :], "pw", -1)
    extended = jnp.concatenate([hartree, upper_plane], axis=1)
    flattened = extended.reshape(-1)
    plane_cells = slab_depth * grid_size
    request = lax.all_to_all(stencil_corner, "pw", split_axis=1, concat_axis=0, tiled=True)
    coord_x = request // plane_cells
    coord_y = request // grid_size % slab_depth
    coord_z = request % grid_size
    gathered = []
    for corner in range(8):
        step_x = corner // 4
        step_y = corner // 2 % 2
        step_z = corner % 2
        cell_index = (
            (coord_x + step_x) % grid_size * (slab_depth + 1) + coord_y + step_y
        ) * grid_size + (coord_z + step_z) % grid_size
        gathered.append(flattened[cell_index])
    stacked = jnp.stack(gathered, axis=0)
    sampled = lax.all_to_all(stacked, "pw", split_axis=1, concat_axis=2, tiled=True)
    summed = jnp.sum(stencil_weight * sampled, axis=0)
    live_slot = jnp.arange(slot_count, dtype=jnp.int32)[None, None, :] < point_count[:, :, None]
    fit_potential = jnp.where(live_slot, summed, 0.0)
    return (local_action, fit_potential)


def solution(mesh):
    placed = (
        P("band", None, "pw", None, None),
        P("pw", None),
        P("band"),
        P(None, "pw", None),
        P("pw", None, None),
        P(None, "pw", None, None),
        P("pw", None),
    )
    return jax.shard_map(
        body,
        mesh=mesh,
        in_specs=placed,
        out_specs=(P("band", None, "pw", None, None), P("pw", None, None)),
        check_vma=False,
    )
```

profile of v0, /device:TPU:8, one launch (start us, length us, event | category | flops | bytes accessed | tf_op | source)
XLA Modules:
  0.0 736.5 jit_solution(2443056056476492475)
XLA Ops:
  11.6 18.7 %all-to-all-start = ((f32[1,2,2,256,256]{4,1,2,0,3:T(2,128)}), f32[1,2,2,256,256]{4,1,2,0,3:T(2,128)S(1)}, u32[]{:S(2)}, u32[]{:S(2)}) async-start(f32[1,2,2,256,256]{4,1,2,0,3:T(2,128)} %copy.52), calls=%async_computation | async-start | bytes 2097152 | tf_op jit(solution)/shard_map/all_to_all | solution.py:88
  31.1 54.5 %all-to-all-done = f32[1,2,2,256,256]{4,1,2,0,3:T(2,128)S(1)} async-done(((f32[1,2,2,256,256]{4,1,2,0,3:T(2,128)}), f32[1,2,2,256,256]{4,1,2,0,3:T(2,128)S(1)}, u32[]{:S(2)}, u32[]{:S(2)}) %all-to-all-start) | async-done | bytes 1048608 | tf_op jit(solution)/shard_map/all_to_all | solution.py:88
  86.4 1.9 convolution_bitcast_fusion
  91.4 29.4 %reduce-scatter.2.cloned.1.call-done = f32[256,4,32]{0,2,1:T(8,128)} async-done(((f32[256,4,256]{0,2,1:T(8,128)}), f32[256,4,32]{0,2,1:T(8,128)}) %reduce-scatter.2.cloned.1.call-update) | async-done | bytes 131088 | tf_op jit(solution)/shard_map/reduce_scatter | solution.py:112
  120.7 2.0 fusion.33
  125.6 16.2 %all-to-all-start.2 = ((f32[64,1,1024]{2,1,0:T(1,128)}), f32[64,1,1024]{2,1,0:T(1,128)}, u32[]{:S(2)}, u32[]{:S(2)}) async-start(f32[64,1,1024]{2,1,0:T(1,128)} %reshape.1541), calls=%async_computation.3 | async-start | bytes 524288 | tf_op jit(solution)/shard_map/all_to_all | solution.py:114
  145.5 15.2 %all-to-all-done.2 = f32[64,1,1024]{2,1,0:T(1,128)} async-done(((f32[64,1,1024]{2,1,0:T(1,128)}), f32[64,1,1024]{2,1,0:T(1,128)}, u32[]{:S(2)}, u32[]{:S(2)}) %all-to-all-start.2) | async-done | bytes 262176 | tf_op jit(solution)/shard_map/all_to_all | solution.py:114
  161.2 2.2 reduce.1
  167.6 2.0 convolution_bitcast_fusion.8
  170.8 3.0 reshape.1543
  173.8 4.5 all-to-all-start.3
  179.2 6.9 all-to-all-done.3
  186.0 2.2 reduce.2
  188.2 1.9 reshape.1544
  190.1 2.8 copy.151
  192.9 1.5 all_to_all.105
  194.5 1.9 fusion.9
  198.4 2.3 reshape.1545
  200.7 10.6 %all_to_all.126 = f32[8,1,8192]{2,1,0:T(1,128)} all-to-all(f32[8,1,8192]{2,1,0:T(1,128)S(1)} %reshape.1545), channel_id=1, replica_groups=mesh['band'=8,'pw'=64] {'band'}, dimensions={0} | all-to-all | bytes 524288 | tf_op jit(solution)/shard_map/all_to_all | solution.py:120
  211.3 6.1 all-to-all-start.6
  217.5 2.2 reduce.3
  219.7 1.9 reshape.1546
  221.6 2.8 copy.150
  224.4 1.5 reshape.1535
  227.4 1.6 copy.76
  229.0 1.8 reshape.1547
  231.0 14.9 %all-to-all-start.5 = ((f32[64,1,1024]{2,1,0:T(1,128)}), f32[64,1,1024]{2,1,0:T(1,128)S(1)}, u32[]{:S(2)}, u32[]{:S(2)}) async-start(f32[64,1,1024]{2,1,0:T(1,128)} %reshape.1547), calls=%async_computation.6 | async-start | bytes 524288 | tf_op jit(solution)/shard_map/all_to_all | solution.py:122
  245.9 1.6 copy.56
  248.8 2.8 fusion.3
  251.6 2.3 copy.58
  253.8 12.9 %all-to-all-done.5 = f32[64,1,1024]{2,1,0:T(1,128)S(1)} async-done(((f32[64,1,1024]{2,1,0:T(1,128)}), f32[64,1,1024]{2,1,0:T(1,128)S(1)}, u32[]{:S(2)}, u32[]{:S(2)}) %all-to-all-start.5) | async-done | bytes 262176 | tf_op jit(solution)/shard_map/all_to_all | solution.py:122
  266.7 6.2 all-to-all-start.1
  276.9 2.4 fusion.11
  279.3 30.2 %all-gather.3.cloned.1.call-done = f32[1,256,4,256]{1,3,2,0:T(8,128)} async-done(((f32[1,256,4,32]{1,3,2,0:T(8,128)}), f32[1,256,4,256]{1,3,2,0:T(8,128)}) %all-gather.3.cloned.1.call-update) | async-done | bytes 1048592 | tf_op jit(solution)/shard_map/all_gather | solution.py:124
  310.5 2.4 collective-permute-start
  314.4 1.5 fusion.94
  315.9 6.3 collective-permute-done
  324.9 45.7 %gather_fusion.7 = f32[8192]{0:T(1024)S(1)} fusion(f32[327680]{0:T(1024)S(1)} %reshape.1420, s32[8192]{0:T(1024)} %get-tuple-element.8), kind=kCustom, calls=%fused_computation.7 | custom fusion | bytes 98304 | tf_op jit(solution)/shard_map/gather | solution.py:141
  370.6 45.5 %gather_fusion.6 = f32[8192]{0:T(1024)S(1)} fusion(f32[327680]{0:T(1024)S(1)} %reshape.1420, s32[8192]{0:T(1024)S(1)} %copy-done.18), kind=kCustom, calls=%fused_computation.6 | custom fusion | bytes 98304 | tf_op jit(solution)/shard_map/gather | solution.py:141
  416.2 45.5 %gather_fusion.5 = f32[8192]{0:T(1024)S(1)} fusion(f32[327680]{0:T(1024)S(1)} %reshape.1420, s32[8192]{0:T(1024)S(1)} %copy-done.17), kind=kCustom, calls=%fused_computation.5 | custom fusion | bytes 98304 | tf_op jit(solution)/shard_map/gather | solution.py:141
  461.7 45.5 %gather_fusion.4 = f32[8192]{0:T(1024)S(1)} fusion(f32[327680]{0:T(1024)S(1)} %reshape.1420, s32[8192]{0:T(1024)S(1)} %copy-done.16), kind=kCustom, calls=%fused_computation.4 | custom fusion | bytes 98304 | tf_op jit(solution)/shard_map/gather | solution.py:141
  507.3 45.5 %gather_fusion.3 = f32[8192]{0:T(1024)S(1)} fusion(f32[327680]{0:T(1024)S(1)} %reshape.1420, s32[8192]{0:T(1024)S(1)} %copy-done.12), kind=kCustom, calls=%fused_computation.3 | custom fusion | bytes 98304 | tf_op jit(solution)/shard_map/gather | solution.py:141
  552.9 45.5 %gather_fusion.2 = f32[8192]{0:T(1024)S(1)} fusion(f32[327680]{0:T(1024)S(1)} %reshape.1420, s32[8192]{0:T(1024)S(1)} %copy-done.15), kind=kCustom, calls=%fused_computation.2 | custom fusion | bytes 98304 | tf_op jit(solution)/shard_map/gather | solution.py:141
  598.4 45.5 %gather_fusion.1 = f32[8192]{0:T(1024)S(1)} fusion(f32[327680]{0:T(1024)S(1)} %reshape.1420, s32[8192]{0:T(1024)S(1)} %copy-done.14), kind=kCustom, calls=%fused_computation.1 | custom fusion | bytes 98304 | tf_op jit(solution)/shard_map/gather | solution.py:141
  644.0 45.5 %gather_fusion = f32[8192]{0:T(1024)S(1)} fusion(f32[327680]{0:T(1024)S(1)} %reshape.1420, s32[8192]{0:T(1024)S(1)} %copy-done.13), kind=kCustom, calls=%fused_computation | custom fusion | bytes 98304 | tf_op jit(solution)/shard_map/gather | solution.py:141
  690.6 16.6 %all-to-all-start.7 = ((f32[8,64,1,128]{3,0,2,1:T(8,128)}), f32[8,64,1,128]{3,0,2,1:T(8,128)S(1)}, u32[]{:S(2)}, u32[]{:S(2)}) async-start(f32[8,64,1,128]{3,0,2,1:T(8,128)} %stack.131), calls=%async_computation.8 | async-start | bytes 524288 | tf_op jit(solution)/shard_map/all_to_all | solution.py:143
  709.7 1.8 convolution_bitcast_fusion.2
  713.3 15.0 %all-to-all-done.7 = f32[8,64,1,128]{3,0,2,1:T(8,128)S(1)} async-done(((f32[8,64,1,128]{3,0,2,1:T(8,128)}), f32[8,64,1,128]{3,0,2,1:T(8,128)S(1)}, u32[]{:S(2)}, u32[]{:S(2)}) %all-to-all-start.7) | async-done | bytes 262176 | tf_op jit(solution)/shard_map/all_to_all | solution.py:143
  (95 shorter events, 41.8 us)
Async XLA Ops:
  7.2 1.5 copy-start.11
  11.6 73.9 %all-to-all-start = ((f32[1,2,2,256,256]{4,1,2,0,3:T(2,128)}), f32[1,2,2,256,256]{4,1,2,0,3:T(2,128)S(1)}, u32[]{:S(2)}, u32[]{:S(2)}) async-start(f32[1,2,2,256,256]{4,1,2,0,3:T(2,128)} %copy.52), calls=%async_computation | async-start | bytes 2097152 | tf_op jit(solution)/shard_map/all_to_all | solution.py:88
  30.4 90.4 %reduce-scatter.2.cloned.1.call-start = ((), (), s32[]{:S(2)}) async-start(), calls=%async_computation.9 | async-start | bytes 1179648 | tf_op jit(solution)/shard_map/reduce_scatter | solution.py:112
  91.4 29.4 %copy-start.9 = (f32[256,1,256]{2,0,1:T(8,128)}, f32[256,1,256]{2,0,1:T(8,128)S(1)}, u32[]{:S(2)}) copy-start(f32[256,1,256]{2,0,1:T(8,128)S(1)} %fusion.57) | copy-start | bytes 786436
  125.6 35.1 %all-to-all-start.2 = ((f32[64,1,1024]{2,1,0:T(1,128)}), f32[64,1,1024]{2,1,0:T(1,128)}, u32[]{:S(2)}, u32[]{:S(2)}) async-start(f32[64,1,1024]{2,1,0:T(1,128)} %reshape.1541), calls=%async_computation.3 | async-start | bytes 524288 | tf_op jit(solution)/shard_map/all_to_all | solution.py:114
  144.0 1.3 copy-start.1
  144.1 1.4 copy-start.3
  166.4 1.2 copy-start
  173.8 12.2 %all-to-all-start.3 = ((f32[8,1,8192]{2,1,0:T(1,128)}), f32[8,1,8192]{2,1,0:T(1,128)}, u32[]{:S(2)}, u32[]{:S(2)}) async-start(f32[8,1,8192]{2,1,0:T(1,128)} %reshape.1543), calls=%async_computation.4 | async-start | bytes 524288 | tf_op jit(solution)/shard_map/all_to_all | solution.py:116
  211.3 19.6 %all-to-all-start.6 = ((s32[1,64,128]{2,0,1:T(1,128)}), s32[1,64,128]{2,0,1:T(1,128)}, u32[]{:S(2)}, u32[]{:S(2)}) async-start(s32[1,64,128]{2,0,1:T(1,128)} %bitcast.297), calls=%async_computation.7 | async-start | bytes 65536 | tf_op jit(solution)/shard_map/all_to_all | solution.py:129
  231.0 35.8 %all-to-all-start.5 = ((f32[64,1,1024]{2,1,0:T(1,128)}), f32[64,1,1024]{2,1,0:T(1,128)S(1)}, u32[]{:S(2)}, u32[]{:S(2)}) async-start(f32[64,1,1024]{2,1,0:T(1,128)} %reshape.1547), calls=%async_computation.6 | async-start | bytes 524288 | tf_op jit(solution)/shard_map/all_to_all | solution.py:122
  248.0 0.7 copy-start.5
  248.0 0.8 copy-start.7
  266.7 423.9 %all-to-all-start.1 = ((f32[1,2,128,4,256]{4,1,3,0,2:T(2,128)}), f32[1,2,128,4,256]{4,1,3,0,2:T(2,128)}, u32[]{:S(2)}, u32[]{:S(2)}) async-start(f32[1,2,128,4,256]{4,1,3,0,2:T(2,128)} %copy.58), calls=%async_computation.1 | async-start | bytes 2097152 | tf_op jit(solution)/shard_map/all_to_all | solution.py:98
  273.0 36.5 %all-gather.3.cloned.1.call-start = ((), (), s32[]{:S(2)}) async-start(), calls=%async_computation.10 | async-start | bytes 1179648 | tf_op jit(solution)/shard_map/all_gather | solution.py:124
  275.7 1.0 copy-start.2
  275.7 1.2 copy-start.4
  310.5 11.8 %collective-permute-start = (f32[256,1,256]{0,2,1:T(8,128)S(1)}, f32[256,1,256]{0,2,1:T(8,128)S(1)}, u32[]{:S(2)}, u32[]{:S(2)}) collective-permute-start(f32[256,1,256]{0,2,1:T(8,128)S(1)} %slice.36), channel_id=1, source_target_pairs={{0,63},{1,0},{2,1},{3,2},{4,3},{5,4},{6,5},{7,6},{8,7},{9,8},{10,9... | collective-permute-start | bytes 786440 | tf_op jit(solution)/shard_map/ppermute | solution.py:14
  324.9 45.7 %copy-start.18 = (s32[8192]{0:T(1024)S(1)}, s32[8192]{0:T(1024)}, u32[]{:S(2)}) copy-start(s32[8192]{0:T(1024)} %get-tuple-element.22) | copy-start | bytes 98308
  370.6 45.6 %copy-start.17 = (s32[8192]{0:T(1024)S(1)}, s32[8192]{0:T(1024)}, u32[]{:S(2)}) copy-start(s32[8192]{0:T(1024)} %get-tuple-element.23) | copy-start | bytes 98308
  416.2 45.6 %copy-start.16 = (s32[8192]{0:T(1024)S(1)}, s32[8192]{0:T(1024)}, u32[]{:S(2)}) copy-start(s32[8192]{0:T(1024)} %get-tuple-element.24) | copy-start | bytes 98308
  461.7 45.6 %copy-start.12 = (s32[8192]{0:T(1024)S(1)}, s32[8192]{0:T(1024)}, u32[]{:S(2)}) copy-start(s32[8192]{0:T(1024)} %get-tuple-element.31) | copy-start | bytes 98308
  507.3 45.6 %copy-start.15 = (s32[8192]{0:T(1024)S(1)}, s32[8192]{0:T(1024)}, u32[]{:S(2)}) copy-start(s32[8192]{0:T(1024)} %get-tuple-element.30) | copy-start | bytes 98308
  552.8 45.6 %copy-start.14 = (s32[8192]{0:T(1024)S(1)}, s32[8192]{0:T(1024)}, u32[]{:S(2)}) copy-start(s32[8192]{0:T(1024)} %get-tuple-element.29) | copy-start | bytes 98308
  598.4 45.6 %copy-start.13 = (s32[8192]{0:T(1024)S(1)}, s32[8192]{0:T(1024)}, u32[]{:S(2)}) copy-start(s32[8192]{0:T(1024)} %get-tuple-element.28) | copy-start | bytes 98308
  690.6 37.7 %all-to-all-start.7 = ((f32[8,64,1,128]{3,0,2,1:T(8,128)}), f32[8,64,1,128]{3,0,2,1:T(8,128)S(1)}, u32[]{:S(2)}, u32[]{:S(2)}) async-start(f32[8,64,1,128]{3,0,2,1:T(8,128)} %stack.131), calls=%async_computation.8 | async-start | bytes 524288 | tf_op jit(solution)/shard_map/all_to_all | solution.py:143
  708.7 1.0 copy-start.6
  708.7 1.0 copy-start.8
  711.5 16.8 %copy-start.10 = (f32[8,1,64,128]{3,2,1,0:T(8,128)S(1)}, f32[8,1,64,128]{3,2,1,0:T(8,128)}, u32[]{:S(2)}) copy-start(f32[8,1,64,128]{3,2,1,0:T(8,128)} %param.12) | copy-start | bytes 786436
  711.5 17.0 %copy-start.19 = (s32[1,64]{1,0:T(1,128)S(1)}, s32[1,64]{1,0:T(1,128)}, u32[]{:S(2)}) copy-start(s32[1,64]{1,0:T(1,128)} %param.13) | copy-start | bytes 772
Sparse Core Ops, SparseCore 0:
  89.5 31.1 reduce-scatter.1
  279.4 29.9 all-gather.2
where the time goes:
time: 746 us; the launch traced here: 737 us
  local copies, waits for them, and re-layouts  411 us (55%)
  waiting for transfers between devices  170 us (23%)
  starting transfers between devices  86.1 us (12%)
  other arithmetic  22.6 us (3%)
  matrix products  19.7 us (3%)
  between operations  15.8 us (2%)
  blocking collectives  10.6 us (1%)
    gather x8, local copies, waits for them, and re-layouts, body(): gathered.append(flattened[cell_index])  364 us
    all_to_all x1, waiting for transfers between devices, body(): lax.all_to_all(partial_section, 'pw', split_axis=3, concat_axis=2, tiled=...  54.5 us
    all_gather x1, waiting for transfers between devices, body(): hartree = lax.all_gather(hartree_part, 'band', axis=2, tiled=True)  30.2 us
    reduce_scatter x1, waiting for transfers between devices, body(): lax.psum_scatter(partial_density, 'band', scatter_dimension=2, tiled=True)  29.4 us
    dot_general x12, matrix products, transform(): lax.dot_general(operand, matrix, (((component_axis, target_axis), (0, 1))...  19.7 us
    unnamed x50, local copies, waits for them, and re-layouts  19.3 us
    all_to_all x1, starting transfers between devices, body(): lax.all_to_all(partial_section, 'pw', split_axis=3, concat_axis=2, tiled=...  18.7 us
    all_to_all x1, starting transfers between devices, body(): lax.all_to_all(stacked, 'pw', split_axis=1, concat_axis=2, tiled=True)  16.6 us
  transfers between devices with their start and end apart: 10, of which 9 were waited for; matrix products, arithmetic and copies ran while one was open for 56% of the time, Pallas kernels for 0%

commit v1 on v0

--- a/solution.py
+++ b/solution.py
@@ -1,3 +1,4 @@
+import functools
 import math
 import jax
 import jax.numpy as jnp
@@ -6,6 +7,23 @@
 
 hartree_scale = 200.0
 exact_mode = lax.Precision.HIGHEST
+
+
+def meet_works(z_in, axis_k):
+    devs = jax.lax.axis_size("band")
+    earlier = [(p - 1, p) for p in range(1, devs)] + [(devs - 1, 0)]
+    q_next = z_in
+    chunks = [q_next]
+    for _ in tuple(range(devs - 1)):
+        q_next = jax.lax.ppermute(q_next, axis_name="band", perm=earlier)
+        chunks += [q_next]
+    current_value = jnp.concatenate([*reversed(chunks)], axis=axis_k)
+    return jnp.roll(
+        current_value, (jax.lax.axis_index("band") + 1) * q_next.shape[axis_k], axis=axis_k
+    )
+
+
+enter_vectors = functools.partial(meet_works, axis_k=2)
 
 
 def shifted(value, axis, steps):
@@ -121,7 +139,7 @@
     spectrum = transform(spectrum, inverse_grid, 2, 0)
     spectrum = lax.all_to_all(spectrum, "pw", split_axis=2, concat_axis=1, tiled=True)
     hartree_part = transform(spectrum, inverse_grid[:, :, 0:1], 1, 0)[0] * inverse_norm
-    hartree = lax.all_gather(hartree_part, "band", axis=2, tiled=True)
+    hartree = enter_vectors(hartree_part)
     upper_plane = shifted(hartree[:, 0:1, :], "pw", -1)
     extended = jnp.concatenate([hartree, upper_plane], axis=1)
     flattened = extended.reshape(-1)

time: 746 us -> 757 us (1.015)
    ppermute x0 -> x7, waiting for transfers between devices: none -> 37.6 us  [meet_works(): q_next = jax.lax.ppermute(q_next, axis_name='band', perm=earlier)]
    all_gather x1 -> x0, waiting for transfers between devices: 30.2 us -> none  [body(): hartree = lax.all_gather(hartree_part, 'band', axis=2, tiled=True)]
    unnamed x50 -> x83, local copies, waits for them, and re-layouts: 19.3 us -> 23.8 us
  transfers between devices with their start and end apart: 10 -> 16, of which waited for: 9 -> 15; matrix products, arithmetic and copies ran while one was open for 56% -> 55% of each run, Pallas kernels for 0% -> 0%
where the time goes in v1:
time: 757 us; the launch traced here: 747 us
  local copies, waits for them, and re-layouts  416 us (55%)
  waiting for transfers between devices  176 us (23%)
  starting transfers between devices  86.2 us (11%)
  other arithmetic  22.4 us (3%)
  matrix products  20 us (3%)
  between operations  16 us (2%)
  blocking collectives  10.6 us (1%)
    gather x8, local copies, waits for them, and re-layouts, body(): gathered.append(flattened[cell_index])  364 us
    all_to_all x1, waiting for transfers between devices, body(): lax.all_to_all(partial_section, 'pw', split_axis=3, concat_axis=2, tiled=...  54.5 us
    ppermute x7, waiting for transfers between devices, meet_works(): q_next = jax.lax.ppermute(q_next, axis_name='band', perm=earlier)  37.6 us
    reduce_scatter x1, waiting for transfers between devices, body(): lax.psum_scatter(partial_density, 'band', scatter_dimension=2, tiled=True)  29.3 us
    unnamed x83, local copies, waits for them, and re-layouts  23.8 us
    dot_general x12, matrix products, transform(): lax.dot_general(operand, matrix, (((component_axis, target_axis), (0, 1))...  20 us
    all_to_all x1, starting transfers between devices, body(): lax.all_to_all(partial_section, 'pw', split_axis=3, concat_axis=2, tiled=...  18.7 us
    all_to_all x1, starting transfers between devices, body(): lax.all_to_all(stacked, 'pw', split_axis=1, concat_axis=2, tiled=True)  17.6 us
  transfers between devices with their start and end apart: 16, of which 15 were waited for; matrix products, arithmetic and copies ran while one was open for 55% of the time, Pallas kernels for 0%

profile of v1, /device:TPU:8, one launch (start us, length us, event | category | flops | bytes accessed | tf_op | source)
XLA Modules:
  0.0 747.0 jit_solution(2600966711890709063)
XLA Ops:
  13.2 18.7 %all-to-all-start = ((f32[1,2,2,256,256]{4,1,2,0,3:T(2,128)}), f32[1,2,2,256,256]{4,1,2,0,3:T(2,128)S(1)}, u32[]{:S(2)}, u32[]{:S(2)}) async-start(f32[1,2,2,256,256]{4,1,2,0,3:T(2,128)} %copy.52), calls=%async_computation | async-start | bytes 2097152 | tf_op jit(solution)/shard_map/all_to_all | solution.py:106
  32.7 54.5 %all-to-all-done = f32[1,2,2,256,256]{4,1,2,0,3:T(2,128)S(1)} async-done(((f32[1,2,2,256,256]{4,1,2,0,3:T(2,128)}), f32[1,2,2,256,256]{4,1,2,0,3:T(2,128)S(1)}, u32[]{:S(2)}, u32[]{:S(2)}) %all-to-all-start) | async-done | bytes 1048608 | tf_op jit(solution)/shard_map/all_to_all | solution.py:106
  88.0 1.9 convolution_bitcast_fusion
  93.0 29.3 %reduce-scatter.2.cloned.1.call-done = f32[256,4,32]{0,2,1:T(8,128)} async-done(((f32[256,4,256]{0,2,1:T(8,128)}), f32[256,4,32]{0,2,1:T(8,128)}) %reduce-scatter.2.cloned.1.call-update) | async-done | bytes 131088 | tf_op jit(solution)/shard_map/reduce_scatter | solution.py:130
  122.3 2.1 fusion.33
  127.2 16.3 %all-to-all-start.2 = ((f32[64,1,1024]{2,1,0:T(1,128)}), f32[64,1,1024]{2,1,0:T(1,128)}, u32[]{:S(2)}, u32[]{:S(2)}) async-start(f32[64,1,1024]{2,1,0:T(1,128)} %reshape.1540), calls=%async_computation.3 | async-start | bytes 524288 | tf_op jit(solution)/shard_map/all_to_all | solution.py:132
  147.2 15.3 %all-to-all-done.2 = f32[64,1,1024]{2,1,0:T(1,128)} async-done(((f32[64,1,1024]{2,1,0:T(1,128)}), f32[64,1,1024]{2,1,0:T(1,128)}, u32[]{:S(2)}, u32[]{:S(2)}) %all-to-all-start.2) | async-done | bytes 262176 | tf_op jit(solution)/shard_map/all_to_all | solution.py:132
  163.0 2.2 reduce.1
  169.0 2.0 convolution_bitcast_fusion.8
  172.2 3.0 reshape.1542
  175.2 4.0 all-to-all-start.3
  179.4 7.4 all-to-all-done.3
  186.8 2.2 reduce.2
  189.0 1.9 reshape.1543
  190.9 2.8 copy.151
  195.2 1.9 fusion.9
  199.2 2.3 reshape.1544
  201.5 10.6 %all_to_all.126 = f32[8,1,8192]{2,1,0:T(1,128)} all-to-all(f32[8,1,8192]{2,1,0:T(1,128)S(1)} %reshape.1544), channel_id=1, replica_groups=mesh['band'=8,'pw'=64] {'band'}, dimensions={0} | all-to-all | bytes 524288 | tf_op jit(solution)/shard_map/all_to_all | solution.py:138
  212.1 6.5 all-to-all-start.6
  218.6 2.2 reduce.3
  220.8 1.9 reshape.1545
  222.7 2.8 copy.150
  232.3 14.8 %all-to-all-start.5 = ((f32[64,1,1024]{2,1,0:T(1,128)}), f32[64,1,1024]{2,1,0:T(1,128)}, u32[]{:S(2)}, u32[]{:S(2)}) async-start(f32[64,1,1024]{2,1,0:T(1,128)} %reshape.1546), calls=%async_computation.6 | async-start | bytes 524288 | tf_op jit(solution)/shard_map/all_to_all | solution.py:140
  250.0 2.8 fusion.3
  252.8 2.3 copy.58
  255.1 12.8 %all-to-all-done.5 = f32[64,1,1024]{2,1,0:T(1,128)} async-done(((f32[64,1,1024]{2,1,0:T(1,128)}), f32[64,1,1024]{2,1,0:T(1,128)}, u32[]{:S(2)}, u32[]{:S(2)}) %all-to-all-start.5) | async-done | bytes 262176 | tf_op jit(solution)/shard_map/all_to_all | solution.py:140
  267.9 6.0 all-to-all-start.1
  273.9 2.2 reduce.4
  280.1 5.6 collective-permute-done
  285.6 5.6 collective-permute-done.1
  291.3 5.6 collective-permute-done.2
  296.9 5.6 collective-permute-done.3
  302.5 5.6 collective-permute-done.4
  308.1 5.6 collective-permute-done.5
  315.2 4.0 collective-permute-done.6
  325.2 2.2 collective-permute-start.7
  328.3 5.2 collective-permute-done.7
  333.6 1.9 copy.80
  337.2 45.5 %gather_fusion.7 = f32[8192]{0:T(1024)S(1)} fusion(f32[327680]{0:T(1024)S(1)} %reshape.1420, s32[8192]{0:T(1024)S(1)} %copy-done.25), kind=kCustom, calls=%fused_computation.7 | custom fusion | bytes 98304 | tf_op jit(solution)/shard_map/gather | solution.py:159
  382.7 45.5 %gather_fusion.6 = f32[8192]{0:T(1024)S(1)} fusion(f32[327680]{0:T(1024)S(1)} %reshape.1420, s32[8192]{0:T(1024)S(1)} %copy-done.27), kind=kCustom, calls=%fused_computation.6 | custom fusion | bytes 98304 | tf_op jit(solution)/shard_map/gather | solution.py:159
  428.3 45.5 %gather_fusion.5 = f32[8192]{0:T(1024)S(1)} fusion(f32[327680]{0:T(1024)S(1)} %reshape.1420, s32[8192]{0:T(1024)S(1)} %copy-done.26), kind=kCustom, calls=%fused_computation.5 | custom fusion | bytes 98304 | tf_op jit(solution)/shard_map/gather | solution.py:159
  473.8 45.5 %gather_fusion.4 = f32[8192]{0:T(1024)S(1)} fusion(f32[327680]{0:T(1024)S(1)} %reshape.1420, s32[8192]{0:T(1024)S(1)} %get-tuple-element.24), kind=kCustom, calls=%fused_computation.4 | custom fusion | bytes 98304 | tf_op jit(solution)/shard_map/gather | solution.py:159
  519.4 45.5 %gather_fusion.3 = f32[8192]{0:T(1024)S(1)} fusion(f32[327680]{0:T(1024)S(1)} %reshape.1420, s32[8192]{0:T(1024)S(1)} %copy-done.24), kind=kCustom, calls=%fused_computation.3 | custom fusion | bytes 98304 | tf_op jit(solution)/shard_map/gather | solution.py:159
  564.9 45.5 %gather_fusion.2 = f32[8192]{0:T(1024)S(1)} fusion(f32[327680]{0:T(1024)S(1)} %reshape.1420, s32[8192]{0:T(1024)S(1)} %get-tuple-element.30), kind=kCustom, calls=%fused_computation.2 | custom fusion | bytes 98304 | tf_op jit(solution)/shard_map/gather | solution.py:159
  610.5 45.5 %gather_fusion.1 = f32[8192]{0:T(1024)S(1)} fusion(f32[327680]{0:T(1024)S(1)} %reshape.1420, s32[8192]{0:T(1024)S(1)} %get-tuple-element.29), kind=kCustom, calls=%fused_computation.1 | custom fusion | bytes 98304 | tf_op jit(solution)/shard_map/gather | solution.py:159
  656.0 45.5 %gather_fusion = f32[8192]{0:T(1024)S(1)} fusion(f32[327680]{0:T(1024)S(1)} %reshape.1420, s32[8192]{0:T(1024)S(1)} %get-tuple-element.28), kind=kCustom, calls=%fused_computation | custom fusion | bytes 98304 | tf_op jit(solution)/shard_map/gather | solution.py:159
  702.6 17.6 %all-to-all-start.7 = ((f32[8,64,1,128]{3,0,2,1:T(8,128)}), f32[8,64,1,128]{3,0,2,1:T(8,128)}, u32[]{:S(2)}, u32[]{:S(2)}) async-start(f32[8,64,1,128]{3,0,2,1:T(8,128)} %stack.131), calls=%async_computation.8 | async-start | bytes 524288 | tf_op jit(solution)/shard_map/all_to_all | solution.py:161
  724.7 13.1 %all-to-all-done.7 = f32[8,64,1,128]{3,0,2,1:T(8,128)} async-done(((f32[8,64,1,128]{3,0,2,1:T(8,128)}), f32[8,64,1,128]{3,0,2,1:T(8,128)}, u32[]{:S(2)}, u32[]{:S(2)}) %all-to-all-start.7) | async-done | bytes 262176 | tf_op jit(solution)/shard_map/all_to_all | solution.py:161
  (141 shorter events, 56.4 us)
Async XLA Ops:
  13.2 73.9 %all-to-all-start = ((f32[1,2,2,256,256]{4,1,2,0,3:T(2,128)}), f32[1,2,2,256,256]{4,1,2,0,3:T(2,128)S(1)}, u32[]{:S(2)}, u32[]{:S(2)}) async-start(f32[1,2,2,256,256]{4,1,2,0,3:T(2,128)} %copy.52), calls=%async_computation | async-start | bytes 2097152 | tf_op jit(solution)/shard_map/all_to_all | solution.py:106
  32.0 90.4 %reduce-scatter.2.cloned.1.call-start = ((), (), s32[]{:S(2)}) async-start(), calls=%async_computation.9 | async-start | bytes 1179648 | tf_op jit(solution)/shard_map/reduce_scatter | solution.py:130
  93.0 29.3 %copy-start.7 = (f32[256,1,256]{2,0,1:T(8,128)}, f32[256,1,256]{2,0,1:T(8,128)S(1)}, u32[]{:S(2)}) copy-start(f32[256,1,256]{2,0,1:T(8,128)S(1)} %fusion.57) | copy-start | bytes 786436
  127.2 35.3 %all-to-all-start.2 = ((f32[64,1,1024]{2,1,0:T(1,128)}), f32[64,1,1024]{2,1,0:T(1,128)}, u32[]{:S(2)}, u32[]{:S(2)}) async-start(f32[64,1,1024]{2,1,0:T(1,128)} %reshape.1540), calls=%async_computation.3 | async-start | bytes 524288 | tf_op jit(solution)/shard_map/all_to_all | solution.py:132
  145.7 1.3 copy-start.1
  145.8 1.3 copy-start.3
  166.7 2.2 copy-start
  175.2 11.6 %all-to-all-start.3 = ((f32[8,1,8192]{2,1,0:T(1,128)}), f32[8,1,8192]{2,1,0:T(1,128)}, u32[]{:S(2)}, u32[]{:S(2)}) async-start(f32[8,1,8192]{2,1,0:T(1,128)} %reshape.1542), calls=%async_computation.4 | async-start | bytes 524288 | tf_op jit(solution)/shard_map/all_to_all | solution.py:134
  212.1 20.2 %all-to-all-start.6 = ((s32[1,64,128]{2,0,1:T(1,128)}), s32[1,64,128]{2,0,1:T(1,128)S(1)}, u32[]{:S(2)}, u32[]{:S(2)}) async-start(s32[1,64,128]{2,0,1:T(1,128)} %bitcast.98), calls=%async_computation.7 | async-start | bytes 65536 | tf_op jit(solution)/shard_map/all_to_all | solution.py:147
  232.3 20.5 %copy-start.21 = (s32[1,64,128]{2,0,1:T(1,128)}, s32[1,64,128]{2,0,1:T(1,128)S(1)}, u32[]{:S(2)}) copy-start(s32[1,64,128]{2,0,1:T(1,128)S(1)} %all-to-all-done.6) | copy-start | bytes 98308
  232.3 35.6 %all-to-all-start.5 = ((f32[64,1,1024]{2,1,0:T(1,128)}), f32[64,1,1024]{2,1,0:T(1,128)}, u32[]{:S(2)}, u32[]{:S(2)}) async-start(f32[64,1,1024]{2,1,0:T(1,128)} %reshape.1546), calls=%async_computation.6 | async-start | bytes 524288 | tf_op jit(solution)/shard_map/all_to_all | solution.py:140
  249.3 0.7 copy-start.5
  267.9 434.7 %all-to-all-start.1 = ((f32[1,2,128,4,256]{4,1,3,0,2:T(2,128)}), f32[1,2,128,4,256]{4,1,3,0,2:T(2,128)S(1)}, u32[]{:S(2)}, u32[]{:S(2)}) async-start(f32[1,2,128,4,256]{4,1,3,0,2:T(2,128)} %copy.58), calls=%async_computation.1 | async-start | bytes 2097152 | tf_op jit(solution)/shard_map/all_to_all | solution.py:116
  277.0 1.0 copy-start.2
  277.0 1.2 copy-start.4
  280.0 5.6 collective-permute-start
  285.6 29.6 %copy-start.8 = (f32[256,4,32]{0,2,1:T(8,128)}, f32[256,4,32]{0,2,1:T(8,128)S(1)}, u32[]{:S(2)}) copy-start(f32[256,4,32]{0,2,1:T(8,128)S(1)} %collective-permute-done) | copy-start | bytes 393220
  285.6 5.6 collective-permute-start.1
  291.2 24.0 %copy-start.10 = (f32[256,4,32]{0,2,1:T(8,128)}, f32[256,4,32]{0,2,1:T(8,128)S(1)}, u32[]{:S(2)}) copy-start(f32[256,4,32]{0,2,1:T(8,128)S(1)} %collective-permute-done.1) | copy-start | bytes 393220
  291.2 5.6 collective-permute-start.2
  296.9 18.3 %copy-start.12 = (f32[256,4,32]{0,2,1:T(8,128)}, f32[256,4,32]{0,2,1:T(8,128)S(1)}, u32[]{:S(2)}) copy-start(f32[256,4,32]{0,2,1:T(8,128)S(1)} %collective-permute-done.2) | copy-start | bytes 393220
  296.9 5.6 collective-permute-start.3
  302.5 12.7 %copy-start.14 = (f32[256,4,32]{0,2,1:T(8,128)}, f32[256,4,32]{0,2,1:T(8,128)S(1)}, u32[]{:S(2)}) copy-start(f32[256,4,32]{0,2,1:T(8,128)S(1)} %collective-permute-done.3) | copy-start | bytes 393220
  302.5 5.6 collective-permute-start.4
  308.1 7.2 copy-start.16
  308.1 5.6 collective-permute-start.5
  313.7 1.6 copy-start.18
  313.7 5.6 collective-permute-start.6
  319.3 5.7 copy-start.19
  319.3 5.7 copy-start.17
  319.3 5.7 copy-start.15
  319.3 5.8 copy-start.13
  319.3 5.8 copy-start.11
  319.3 5.8 copy-start.9
  320.3 7.1 copy-start.22
  325.2 8.3 %collective-permute-start.7 = (f32[256,1,256]{0,2,1:T(8,128)S(1)}, f32[256,1,256]{0,2,1:T(8,128)S(1)}, u32[]{:S(2)}, u32[]{:S(2)}) collective-permute-start(f32[256,1,256]{0,2,1:T(8,128)S(1)} %constant_dynamic-slice_fusion), channel_id=1, source_target_pairs={{0,63},{1,0},{2,1},{3,2},{4,3},{5,4},{6,5},{7,6},{8,7},{9,8},{10,9... | collective-permute-start | bytes 786440 | tf_op jit(solution)/shard_map/ppermute | solution.py:32
  335.5 1.7 copy-start.25
  337.1 45.6 %copy-start.27 = (s32[8192]{0:T(1024)S(1)}, s32[8192]{0:T(1024)}, u32[]{:S(2)}) copy-start(s32[8192]{0:T(1024)} %get-tuple-element.22) | copy-start | bytes 98308
  382.7 45.6 %copy-start.26 = (s32[8192]{0:T(1024)S(1)}, s32[8192]{0:T(1024)}, u32[]{:S(2)}) copy-start(s32[8192]{0:T(1024)} %get-tuple-element.23) | copy-start | bytes 98308
  473.8 45.6 %copy-start.24 = (s32[8192]{0:T(1024)S(1)}, s32[8192]{0:T(1024)}, u32[]{:S(2)}) copy-start(s32[8192]{0:T(1024)} %get-tuple-element.31) | copy-start | bytes 98308
  702.6 35.2 %all-to-all-start.7 = ((f32[8,64,1,128]{3,0,2,1:T(8,128)}), f32[8,64,1,128]{3,0,2,1:T(8,128)}, u32[]{:S(2)}, u32[]{:S(2)}) async-start(f32[8,64,1,128]{3,0,2,1:T(8,128)} %stack.131), calls=%async_computation.8 | async-start | bytes 524288 | tf_op jit(solution)/shard_map/all_to_all | solution.py:161
  720.2 1.0 copy-start.6
  720.5 2.5 copy-start.20
  721.1 16.7 %copy-start.23 = (f32[8,1,64,128]{3,2,1,0:T(8,128)S(1)}, f32[8,1,64,128]{3,2,1,0:T(8,128)}, u32[]{:S(2)}) copy-start(f32[8,1,64,128]{3,2,1,0:T(8,128)} %param.12) | copy-start | bytes 786436
  721.2 17.8 %copy-start.28 = (s32[1,64]{1,0:T(1,128)S(1)}, s32[1,64]{1,0:T(1,128)}, u32[]{:S(2)}) copy-start(s32[1,64]{1,0:T(1,128)} %param.13) | copy-start | bytes 772
Sparse Core Ops, SparseCore 0:
  91.1 31.1 reduce-scatter.1
